TPU v7x, 256 devices: a whole 4x4x8 slice. The times are simulated.
256 devices in a mesh: expert: 32 (over z, x), dp: 8 (over y, core).
Axes of the slice: x: 4, y: 4, z: 8, core: 2. Of those that a mesh axis runs over, the one named last changes fastest.
Arguments:
- tokens: bfloat16 [3072, 4096], P('expert', 'dp'), may hold values from -6 to 6
- route_weight: float32 [3072, 8], P('expert'), may hold values from 0.05 to 0.25
- route_expert: int32 [3072, 8], P('expert'), may hold values from 0 to 31, all different within a row; in each aligned block of 96 rows (0 to 95, 96 to 191, ...) at most 32 rows name the same one
- cotangent: bfloat16 [3072, 4096], P('expert', 'dp'), may hold values from -6 to 6
- gate_quant: bfloat16 [32, 4096, 1024], P('expert', None, 'dp'), may hold values from -0.09375 to 0.09375
- up_quant: bfloat16 [32, 4096, 1024], P('expert', None, 'dp'), may hold values from -0.09375 to 0.09375
- gate_scale: float32 [32, 32, 8], P('expert', None, 'dp'), may hold values from 0.5 to 2
- up_scale: float32 [32, 32, 8], P('expert', None, 'dp'), may hold values from 0.5 to 2
- down_quant: bfloat16 [32, 1024, 4096], P('expert', None, 'dp'), may hold values from -0.1875 to 0.1875
- down_scale: float32 [32, 8, 32], P('expert', None, 'dp'), may hold values from 0.5 to 2
- first_moment: float32 [32, 1024, 4096], P('expert', None, 'dp'), may hold values from -6 to 6
- second_moment: float32 [32, 1024, 4096], P('expert', None, 'dp'), may hold values from 0.5 to 8
- old_expert: int32 [32], replicated, may hold values from 0 to 31, each once
- new_holder: int32 [32], replicated, may hold values from 0 to 31, each once
Outputs:
- mixed: bfloat16 [3072, 4096], P('expert', 'dp')
- new_down: bfloat16 [32, 1024, 4096], P('expert', None, 'dp')
- new_first: float32 [32, 1024, 4096], P('expert', None, 'dp')
- new_second: float32 [32, 1024, 4096], P('expert', None, 'dp')
Inputs may be any that keep to these rules, and one draw needn't show every extreme that they name: `route_expert`: within each aligned block of 96 tokens (the tokens of one index of expert) no expert is named by more than 32 routes, a bound that some block reaches; a token names 8 different experts. `old_expert`: A permutation of the experts. `new_holder`: A permutation of the indices of expert.
All inputs are finite; a program needn't handle non-finite values.
Results may differ from a plain program's by a relative error of at most 0.0076.
Values may be sent and summed in bfloat16 or wider, within the bound.
A program may use at most 128 MiB of HBM per device.

v0:
```python
import jax
import jax.numpy as jnp
from jax import lax
from jax.sharding import PartitionSpec as P

QB = 128
beta_first = 0.9
beta_second = 0.95
adam_eps = 1e-08
learn_rate = 0.003
decay_rate = 0.1
step_count = 20


def dequantize(quant, scale):
    tiled = jnp.repeat(jnp.repeat(scale, QB, axis=0), QB, axis=1)
    return quant.astype(jnp.float32) * tiled


def adam_step(master, grad, first, second):
    first_new = beta_first * first + (1.0 - beta_first) * grad
    second_new = beta_second * second + (1.0 - beta_second) * grad * grad
    fix_first = 1.0 - beta_first**step_count
    fix_second = 1.0 - beta_second**step_count
    update = first_new / fix_first / (jnp.sqrt(second_new / fix_second) + adam_eps)
    fresh = (master - learn_rate * (update + decay_rate * master)).astype(jnp.bfloat16)
    return (fresh, first_new, second_new)


def holder_tables(old_expert, new_holder):
    number = old_expert.shape[0]
    labels = jnp.arange(number, dtype=jnp.int32)
    holds = (old_expert[:, None] == labels[None, :]).astype(jnp.int32)
    old_device = jnp.sum(holds * labels[:, None], axis=0)
    new_device = jnp.sum(holds * new_holder[:, None], axis=0)
    takes = (new_holder[:, None] == labels[None, :]).astype(jnp.int32)
    giver = jnp.sum(takes * labels[:, None], axis=0)
    return (old_device, new_device, giver)


def pack_rows(arrays, number):
    lines = []
    for array_item in arrays:
        line = array_item.reshape(-1)
        lines.append(line.reshape(number, -1))
    return jnp.concatenate(lines, axis=1)


def unpack_rows(packed, arrays):
    number = packed.shape[0]
    result = []
    offset = 0
    for array_item in arrays:
        span_cols = -(-array_item.size // number)
        block_rows = packed[:, offset : offset + span_cols]
        result.append(block_rows.reshape(-1).reshape(array_item.shape))
        offset = offset + span_cols
    return tuple(result)


def move_weights(arrays, giver):
    packed = pack_rows(arrays, giver.shape[0])
    spread = lax.all_to_all(packed, "expert", split_axis=0, concat_axis=0, tiled=True)
    settled = lax.all_to_all(
        jnp.take(spread, giver, axis=0), "expert", split_axis=0, concat_axis=0, tiled=True
    )
    return unpack_rows(settled, arrays)


def move_state(arrays, giver):
    packed = pack_rows(arrays, giver.shape[0])
    spread = lax.all_to_all(packed, "expert", split_axis=0, concat_axis=0, tiled=True)
    settled = lax.all_to_all(
        jnp.take(spread, giver, axis=0), "expert", split_axis=0, concat_axis=0, tiled=True
    )
    return unpack_rows(settled, arrays)


def plan_slots(route_expert, target_of, number, capacity):
    route_total = route_expert.shape[0] * route_expert.shape[1]
    flat_expert = route_expert.reshape(-1)
    labels = jnp.arange(number, dtype=jnp.int32)
    pick = (flat_expert[:, None] == labels[None, :]).astype(jnp.int32)
    target = jnp.sum(pick * target_of[None, :], axis=1)
    onehot = (target[:, None] == labels[None, :]).astype(jnp.int32)
    earlier = jnp.cumsum(onehot, axis=0) - onehot
    slot_index = jnp.sum(earlier * onehot, axis=1)
    route_place = target * capacity + slot_index
    slot_route = (
        jnp.full((number * capacity,), -1, jnp.int32)
        .at[route_place]
        .set(jnp.arange(route_total, dtype=jnp.int32))
    )
    return (route_place, slot_route)


def per_device(
    tokens,
    route_weight,
    route_expert,
    cotangent,
    gate_quant,
    up_quant,
    gate_scale,
    up_scale,
    down_quant,
    down_scale,
    first_moment,
    second_moment,
    old_expert,
    new_holder,
):
    number = lax.axis_size("expert")
    tok_rows, top_count = route_expert.shape
    model_width = gate_quant.shape[1]
    column_width = cotangent.shape[1]
    capacity = min(tok_rows, tok_rows * top_count // number * 4 // 3)
    old_device, new_device, giver = holder_tables(old_expert, new_holder)
    gate_quant, up_quant, down_quant = move_weights((gate_quant, up_quant, down_quant), giver)
    gate_scale, up_scale, down_scale, first_moment, second_moment = move_state(
        (gate_scale, up_scale, down_scale, first_moment, second_moment), giver
    )
    route_place, slot_route = plan_slots(route_expert, new_device, number, capacity)
    live_rows = slot_route >= 0
    safe_route = jnp.maximum(slot_route, 0)
    token_ids = safe_route // top_count
    weight_rows = jnp.where(
        live_rows, jnp.take(route_weight.reshape(-1), safe_route), jnp.float32(0.0)
    )
    back_rows = (
        weight_rows[:, None] * jnp.take(cotangent, token_ids, axis=0).astype(jnp.float32)
    ).astype(jnp.bfloat16)
    back_send = back_rows.reshape(number, capacity, column_width)
    whole_tokens = lax.all_gather(tokens, "dp", axis=1, tiled=True)
    sent_rows = jnp.take(whole_tokens, token_ids, axis=0).reshape(number, capacity, model_width)
    arrived, back_in = (
        lax.all_to_all(sent_rows, "expert", split_axis=0, concat_axis=0, tiled=True),
        lax.all_to_all(back_send, "expert", split_axis=0, concat_axis=0, tiled=True),
    )
    rows_in = arrived.reshape(-1, model_width)
    back_in = back_in.reshape(-1, column_width)
    gate_w = dequantize(gate_quant[0], gate_scale[0]).astype(jnp.bfloat16)
    up_w = dequantize(up_quant[0], up_scale[0]).astype(jnp.bfloat16)
    master = dequantize(down_quant[0], down_scale[0])
    down_w = master.astype(jnp.bfloat16)
    gate_val = jnp.dot(rows_in, gate_w, preferred_element_type=jnp.float32)
    up_val = jnp.dot(rows_in, up_w, preferred_element_type=jnp.float32)
    hidden_part = (jax.nn.silu(gate_val) * up_val).astype(jnp.bfloat16)
    hidden_full = lax.all_gather(hidden_part, "dp", axis=1, tiled=True)
    out_total = jnp.dot(hidden_full, down_w, preferred_element_type=jnp.float32)
    grad_total = lax.dot_general(
        hidden_full, back_in, (((0,), (0,)), ((), ())), preferred_element_type=jnp.float32
    )
    out_rows = out_total.astype(jnp.bfloat16).reshape(number, capacity, column_width)
    returned = lax.all_to_all(out_rows, "expert", split_axis=0, concat_axis=0, tiled=True).reshape(
        -1, column_width
    )
    picked = (
        jnp.take(returned, route_place, axis=0)
        .reshape(tok_rows, top_count, column_width)
        .astype(jnp.float32)
    )
    mixed = jnp.sum(picked * route_weight[:, :, None], axis=1).astype(jnp.bfloat16)
    fresh, first_new, second_new = adam_step(master, grad_total, first_moment[0], second_moment[0])
    fresh = fresh[None]
    first_new = first_new[None]
    second_new = second_new[None]
    return (mixed, fresh, first_new, second_new)


def solution(mesh):
    in_specs = (
        P("expert", "dp"),
        P("expert", None),
        P("expert", None),
        P("expert", "dp"),
        P("expert", None, "dp"),
        P("expert", None, "dp"),
        P("expert", None, "dp"),
        P("expert", None, "dp"),
        P("expert", None, "dp"),
        P("expert", None, "dp"),
        P("expert", None, "dp"),
        P("expert", None, "dp"),
        P(),
        P(),
    )
    out_specs = (
        P("expert", "dp"),
        P("expert", None, "dp"),
        P("expert", None, "dp"),
        P("expert", None, "dp"),
    )
    return jax.shard_map(
        per_device, mesh=mesh, in_specs=in_specs, out_specs=out_specs, check_vma=False
    )
```

profile of v0, /device:TPU:2, one launch (start us, length us, event | category | flops | bytes accessed | tf_op | source)
XLA Modules:
  0.0 698.2 jit_solution(656383670032208674)
XLA Ops:
  7.2 2.4 reshape_reshape.24
  14.7 3.8 reduce.10
  18.5 5.4 reshape.303
  23.9 11.8 %all-to-all-start.1 = ((bf16[32,2,24576]{2,1,0:T(2,128)(2,1)}), bf16[32,2,24576]{2,1,0:T(2,128)(2,1)S(1)}, u32[]{:S(2)}, u32[]{:S(2)}) async-start(bf16[32,2,24576]{2,1,0:T(2,128)(2,1)} %reshape.303), calls=%async_computation.1 | async-start | bytes 6291456 | tf_op jit(solution)/shard_map/all_to_all | solution.py:63
  36.0 2.7 reshape_reshape.30
  38.7 2.7 reshape_reshape.31
  45.6 9.3 %dynamic-update-slice.3 = f32[32,32771]{1,0:T(8,128)} dynamic-update-slice(f32[32,32771]{1,0:T(8,128)} %dynamic-update-slice.2, f32[32,16384]{1,0:T(8,128)} %reshape_reshape.30, s32[]{} %constant.150, s32[]{} %constant.153) | dynamic-update-slice | bytes 4194308
  54.9 8.7 %dynamic-update-slice.4 = f32[32,32771]{1,0:T(8,128)} dynamic-update-slice(f32[32,32771]{1,0:T(8,128)} %dynamic-update-slice.3, f32[32,16384]{1,0:T(8,128)} %reshape_reshape.31, s32[]{} %constant.150, s32[]{} %constant.154) | dynamic-update-slice | bytes 4194308 | tf_op jit(solution)/shard_map/concatenate | solution.py:46
  63.5 9.8 %all_to_all.43 = f32[32,1,32771]{2,1,0:T(1,128)} reshape(f32[32,32771]{1,0:T(8,128)} %dynamic-update-slice.4) | data formatting | bytes 8389376 | tf_op jit(solution)/shard_map/all_to_all | solution.py:72
  73.5 33.4 %all-to-all-done.1 = bf16[32,2,24576]{2,1,0:T(2,128)(2,1)S(1)} async-done(((bf16[32,2,24576]{2,1,0:T(2,128)(2,1)}), bf16[32,2,24576]{2,1,0:T(2,128)(2,1)S(1)}, u32[]{:S(2)}, u32[]{:S(2)}) %all-to-all-start.1) | async-done | bytes 3145760 | tf_op jit(solution)/shard_map/all_to_all | solution.py:63
  106.9 7.8 %all-to-all-start.3 = ((f32[32,1,32771]{2,1,0:T(1,128)}), f32[32,1,32771]{2,1,0:T(1,128)}, u32[]{:S(2)}, u32[]{:S(2)}) async-start(f32[32,1,32771]{2,1,0:T(1,128)} %all_to_all.43), calls=%async_computation.3 | async-start | bytes 8421376 | tf_op jit(solution)/shard_map/all_to_all | solution.py:72
  114.7 12.4 %reshape.304 = bf16[32,1,49152]{2,1,0:T(2,128)(2,1)} reshape(bf16[32,2,24576]{2,1,0:T(2,128)(2,1)S(1)} %all-to-all-done.1) | data formatting | bytes 6291456
  127.2 6.2 copy.83
  133.4 4.3 gather_fusion.1
  139.9 3.7 reduce.11
  143.7 5.4 reshape.305
  149.1 59.0 %all-to-all-done.3 = f32[32,1,32771]{2,1,0:T(1,128)} async-done(((f32[32,1,32771]{2,1,0:T(1,128)}), f32[32,1,32771]{2,1,0:T(1,128)}, u32[]{:S(2)}, u32[]{:S(2)}) %all-to-all-start.3) | async-done | bytes 4194720 | tf_op jit(solution)/shard_map/all_to_all | solution.py:72
  208.1 8.3 %all-to-all-start.2 = ((bf16[32,2,24576]{2,1,0:T(2,128)(2,1)}), bf16[32,2,24576]{2,1,0:T(2,128)(2,1)}, u32[]{:S(2)}, u32[]{:S(2)}) async-start(bf16[32,2,24576]{2,1,0:T(2,128)(2,1)} %reshape.305), calls=%async_computation.2 | async-start | bytes 6291456 | tf_op jit(solution)/shard_map/all_to_all | solution.py:64
  216.5 4.4 copy.81
  220.9 7.6 %gather_fusion.2 = f32[32,32771]{1,0:T(8,128)} fusion(f32[32,32771]{1,0:T(8,128)} %bitcast.77, s32[1024]{0:T(1024)S(1)} %pad_clamp_fusion.1), kind=kCustom, calls=%fused_computation.2 | custom fusion | bytes 8389504 | tf_op jit(solution)/shard_map/jit(_take)/gather | solution.py:74
  228.5 2.5 bitcast_select_fusion
  231.0 6.3 copy.60
  237.3 50.3 %all-to-all-done.2 = bf16[32,2,24576]{2,1,0:T(2,128)(2,1)} async-done(((bf16[32,2,24576]{2,1,0:T(2,128)(2,1)}), bf16[32,2,24576]{2,1,0:T(2,128)(2,1)}, u32[]{:S(2)}, u32[]{:S(2)}) %all-to-all-start.2) | async-done | bytes 3145760 | tf_op jit(solution)/shard_map/all_to_all | solution.py:64
  287.6 7.4 %all-to-all-start.4 = ((f32[32,1,32771]{2,1,0:T(1,128)}), f32[32,1,32771]{2,1,0:T(1,128)}, u32[]{:S(2)}, u32[]{:S(2)}) async-start(f32[32,1,32771]{2,1,0:T(1,128)} %copy.60), calls=%async_computation.4 | async-start | bytes 8421376 | tf_op jit(solution)/shard_map/all_to_all | solution.py:73
  297.5 3.4 scatter_custom_fusion
  301.0 14.1 %all_gather.6 = bf16[96,4096]{1,0:T(8,128)(2,1)S(1)} all-gather(bf16[96,512]{1,0:T(8,128)(2,1)S(1)} %copy-done.7), channel_id=1, replica_groups=mesh['expert'=32,'dp'=8] {'dp'}, dimensions={1}, use_global_device_ids=true | all-gather | bytes 884736 | tf_op jit(solution)/shard_map/all_gather | solution.py:134
  315.1 7.8 %gather_fusion = bf16[1024,4096]{1,0:T(8,128)(2,1)} fusion(bf16[96,4096]{1,0:T(8,128)(2,1)S(1)} %all_gather.6, s32[1024]{0:T(1024)S(1)} %get-tuple-element.17), kind=kCustom, calls=%fused_computation | custom fusion | bytes 16781312 | tf_op jit(solution)/shard_map/jit(_take)/gather | solution.py:135
  322.9 7.4 %broadcast_select_fusion = bf16[32,32,4096]{2,1,0:T(8,128)(2,1)} fusion(bf16[32,32,4096]{2,1,0:T(8,128)(2,1)} %bitcast.80, pred[32,32]{1,0:T(8,128)(4,1)S(1)} %broadcast_in_dim.103), kind=kLoop, calls=%fused_computation.7 | loop fusion | flops 4194304 | bytes 16778240 | tf_op jit(solution)/shard_map/jit(_take)/select_n | solution.py:135
  330.3 58.3 %all-to-all-done.4 = f32[32,1,32771]{2,1,0:T(1,128)} async-done(((f32[32,1,32771]{2,1,0:T(1,128)}), f32[32,1,32771]{2,1,0:T(1,128)}, u32[]{:S(2)}, u32[]{:S(2)}) %all-to-all-start.4) | async-done | bytes 4194720 | tf_op jit(solution)/shard_map/all_to_all | solution.py:73
  388.7 7.7 %all-to-all-start = ((bf16[32,32,4096]{2,1,0:T(8,128)(2,1)}), bf16[32,32,4096]{2,1,0:T(8,128)(2,1)}, u32[]{:S(2)}, u32[]{:S(2)}) async-start(bf16[32,32,4096]{2,1,0:T(8,128)(2,1)} %broadcast_select_fusion), calls=%async_computation | async-start | bytes 16777216 | tf_op jit(solution)/shard_map/all_to_all | solution.py:137
  396.6 4.5 gather_fusion.4
  401.2 4.0 gather_fusion.5
  406.5 18.9 %reshape.306 = bf16[32,1,49152]{2,1,0:T(2,128)(2,1)} reshape(bf16[32,2,24576]{2,1,0:T(2,128)(2,1)} %all-to-all-done.2) | data formatting | bytes 6291456
  425.4 6.2 copy.82
  431.7 2.5 copy.80
  436.7 2.3 convert_element_type.66
  439.1 2.3 convert_element_type.69
  441.4 145.2 %all-to-all-done = bf16[32,32,4096]{2,1,0:T(8,128)(2,1)} async-done(((bf16[32,32,4096]{2,1,0:T(8,128)(2,1)}), bf16[32,32,4096]{2,1,0:T(8,128)(2,1)}, u32[]{:S(2)}, u32[]{:S(2)}) %all-to-all-start) | async-done | bytes 8388640 | tf_op jit(solution)/shard_map/all_to_all | solution.py:137
  586.6 13.2 %all-to-all-start.6 = ((bf16[32,32,512]{2,1,0:T(8,128)(2,1)}), bf16[32,32,512]{2,1,0:T(8,128)(2,1)}, u32[]{:S(2)}, u32[]{:S(2)}) async-start(bf16[32,32,512]{2,1,0:T(8,128)(2,1)} %multiply_convert_fusion), calls=%async_computation.6 | async-start | bytes 2097152 | tf_op jit(solution)/shard_map/all_to_all | solution.py:138
  600.1 6.0 fusion.15
  606.1 6.4 fusion.1
  615.9 27.8 %all-gather.2.cloned.1.call-done = bf16[1024,1024]{1,0:T(8,128)(2,1)} async-done(((bf16[1024,128]{1,0:T(8,128)(2,1)}), bf16[1024,1024]{1,0:T(8,128)(2,1)}) %all-gather.2.cloned.1.call-update) | async-done | bytes 2097168 | tf_op jit(solution)/shard_map/all_gather | solution.py:149
  648.5 10.1 %all-to-all-start.5 = ((bf16[32,32,512]{2,1,0:T(8,128)(2,1)}), bf16[32,32,512]{2,1,0:T(8,128)(2,1)S(1)}, u32[]{:S(2)}, u32[]{:S(2)}) async-start(bf16[32,32,512]{2,1,0:T(8,128)(2,1)} %bitcast.12), calls=%async_computation.5 | async-start | bytes 2097152 | tf_op jit(solution)/shard_map/all_to_all | solution.py:155
  658.7 4.7 slice_multiply_fusion
  663.4 2.7 mul.139
  667.6 9.3 %fusion.5 = (f32[1,1024,512]{2,1,0:T(8,128)}, bf16[1,1024,512]{2,1,0:T(8,128)(2,1)}, f32[1,1024,512]{2,1,0:T(8,128)}) fusion(f32[1024,512]{1,0:T(8,128)} %mul.146, f32[1024,512]{1,0:T(8,128)} %mul.139, f32[1024,512]{1,0:T(8,128)} %copy-done.3, f32[128,8,4,128]{3,2,1,0:T(4,128)} %bitcast.87, bf16[1024,1024]{1,0:T(8,128)(2,1)} %all-gather.2.cloned.1.call-done, ...), kind=kOutput, calls=%fused_computation.34 | convolution fusion | flops 1081606144 | bytes 16777216 | tf_op jit(solution)/shard_map/dot_general | solution.py:151
  676.9 10.2 %all-to-all-done.5 = bf16[32,32,512]{2,1,0:T(8,128)(2,1)S(1)} async-done(((bf16[32,32,512]{2,1,0:T(8,128)(2,1)}), bf16[32,32,512]{2,1,0:T(8,128)(2,1)S(1)}, u32[]{:S(2)}, u32[]{:S(2)}) %all-to-all-start.5) | async-done | bytes 1048608 | tf_op jit(solution)/shard_map/all_to_all | solution.py:155
  687.2 2.7 gather_fusion.3
  (84 shorter events, 29.9 us)
Async XLA Ops:
  7.2 394.1 %copy-start = (bf16[96,512]{1,0:T(8,128)(2,1)S(1)}, bf16[96,512]{1,0:T(8,128)(2,1)}, u32[]{:S(2)}) copy-start(bf16[96,512]{1,0:T(8,128)(2,1)} %param.17) | copy-start | bytes 294916
  7.2 2.5 copy-start.4
  7.2 3.7 copy-start.5
  23.9 11.8 %copy-start.11 = (f32[1,32,1]{1,2,0:T(1,128)S(1)}, f32[1,32,1]{1,2,0:T(1,128)}, u32[]{:S(2)}) copy-start(f32[1,32,1]{1,2,0:T(1,128)} %param.20) | copy-start | bytes 388
  23.9 11.9 %copy-start.12 = (f32[1,32,1]{1,2,0:T(1,128)S(1)}, f32[1,32,1]{1,2,0:T(1,128)}, u32[]{:S(2)}) copy-start(f32[1,32,1]{1,2,0:T(1,128)} %param.21) | copy-start | bytes 388
  23.9 12.0 %copy-start.10 = (f32[1,8,4]{1,2,0:T(4,128)S(1)}, f32[1,8,4]{1,2,0:T(4,128)}, u32[]{:S(2)}) copy-start(f32[1,8,4]{1,2,0:T(4,128)} %param.23) | copy-start | bytes 388
  23.9 83.0 %all-to-all-start.1 = ((bf16[32,2,24576]{2,1,0:T(2,128)(2,1)}), bf16[32,2,24576]{2,1,0:T(2,128)(2,1)S(1)}, u32[]{:S(2)}, u32[]{:S(2)}) async-start(bf16[32,2,24576]{2,1,0:T(2,128)(2,1)} %reshape.303), calls=%async_computation.1 | async-start | bytes 6291456 | tf_op jit(solution)/shard_map/all_to_all | solution.py:63
  63.5 9.8 %copy-start.13 = (s32[32]{0:T(128)S(1)}, s32[32]{0:T(128)}, u32[]{:S(2)}) copy-start(s32[32]{0:T(128)} %param.27) | copy-start | bytes 388
  63.5 9.8 %copy-start.14 = (s32[32]{0:T(128)S(1)}, s32[32]{0:T(128)}, u32[]{:S(2)}) copy-start(s32[32]{0:T(128)} %param.26) | copy-start | bytes 388
  106.9 101.2 %all-to-all-start.3 = ((f32[32,1,32771]{2,1,0:T(1,128)}), f32[32,1,32771]{2,1,0:T(1,128)}, u32[]{:S(2)}, u32[]{:S(2)}) async-start(f32[32,1,32771]{2,1,0:T(1,128)} %all_to_all.43), calls=%async_computation.3 | async-start | bytes 8421376 | tf_op jit(solution)/shard_map/all_to_all | solution.py:72
  208.1 79.5 %all-to-all-start.2 = ((bf16[32,2,24576]{2,1,0:T(2,128)(2,1)}), bf16[32,2,24576]{2,1,0:T(2,128)(2,1)}, u32[]{:S(2)}, u32[]{:S(2)}) async-start(bf16[32,2,24576]{2,1,0:T(2,128)(2,1)} %reshape.305), calls=%async_computation.2 | async-start | bytes 6291456 | tf_op jit(solution)/shard_map/all_to_all | solution.py:64
  237.3 57.7 %copy-start.8 = (s32[96,8]{0,1:T(8,128)S(1)}, s32[96,8]{0,1:T(8,128)}, u32[]{:S(2)}) copy-start(s32[96,8]{0,1:T(8,128)} %param.16) | copy-start | bytes 9220
  237.3 63.7 %copy-start.7 = (bf16[96,512]{1,0:T(8,128)(2,1)S(1)}, bf16[96,512]{1,0:T(8,128)(2,1)}, u32[]{:S(2)}) copy-start(bf16[96,512]{1,0:T(8,128)(2,1)} %param.14) | copy-start | bytes 294916
  287.6 101.0 %all-to-all-start.4 = ((f32[32,1,32771]{2,1,0:T(1,128)}), f32[32,1,32771]{2,1,0:T(1,128)}, u32[]{:S(2)}, u32[]{:S(2)}) async-start(f32[32,1,32771]{2,1,0:T(1,128)} %copy.60), calls=%async_computation.4 | async-start | bytes 8421376 | tf_op jit(solution)/shard_map/all_to_all | solution.py:73
  330.3 66.1 %copy-start.9 = (f32[96,8]{0,1:T(8,128)S(1)}, f32[96,8]{0,1:T(8,128)}, u32[]{:S(2)}) copy-start(f32[96,8]{0,1:T(8,128)} %param.15) | copy-start | bytes 9220
  388.7 198.0 %all-to-all-start = ((bf16[32,32,4096]{2,1,0:T(8,128)(2,1)}), bf16[32,32,4096]{2,1,0:T(8,128)(2,1)}, u32[]{:S(2)}, u32[]{:S(2)}) async-start(bf16[32,32,4096]{2,1,0:T(8,128)(2,1)} %broadcast_select_fusion), calls=%async_computation | async-start | bytes 16777216 | tf_op jit(solution)/shard_map/all_to_all | solution.py:137
  434.1 2.6 copy-start.1
  586.6 61.9 %all-to-all-start.6 = ((bf16[32,32,512]{2,1,0:T(8,128)(2,1)}), bf16[32,32,512]{2,1,0:T(8,128)(2,1)}, u32[]{:S(2)}, u32[]{:S(2)}) async-start(bf16[32,32,512]{2,1,0:T(8,128)(2,1)} %multiply_convert_fusion), calls=%async_computation.6 | async-start | bytes 2097152 | tf_op jit(solution)/shard_map/all_to_all | solution.py:138
  599.8 43.9 %all-gather.2.cloned.1.call-start = ((), (), s32[]{:S(2)}) async-start(), calls=%async_computation.7 | async-start | bytes 2359296 | tf_op jit(solution)/shard_map/all_gather | solution.py:149
  600.1 6.0 copy-start.6
  615.8 32.8 %copy-start.3 = (f32[1024,512]{1,0:T(8,128)}, f32[1024,512]{1,0:T(8,128)S(1)}, u32[]{:S(2)}) copy-start(f32[1024,512]{1,0:T(8,128)S(1)} %reshape.234) | copy-start | bytes 6291460
  643.6 2.6 copy-start.15
  644.9 1.3 copy-start.2
  648.5 38.6 %all-to-all-start.5 = ((bf16[32,32,512]{2,1,0:T(8,128)(2,1)}), bf16[32,32,512]{2,1,0:T(8,128)(2,1)S(1)}, u32[]{:S(2)}, u32[]{:S(2)}) async-start(bf16[32,32,512]{2,1,0:T(8,128)(2,1)} %bitcast.12), calls=%async_computation.5 | async-start | bytes 2097152 | tf_op jit(solution)/shard_map/all_to_all | solution.py:155
Sparse Core Ops, SparseCore 0:
  612.7 30.9 all-gather.1
where the time goes:
time: 706 us; the launch traced here: 698 us
  waiting for transfers between devices  384 us (54%)
  local copies, waits for them, and re-layouts  160 us (23%)
  starting transfers between devices  66.5 us (9%)
  other arithmetic  34.7 us (5%)
  matrix products  24 us (3%)
  between operations  14.6 us (2%)
  blocking collectives  14.1 us (2%)
    all_to_all x1, waiting for transfers between devices, per_device(): lax.all_to_all(sent_rows, 'expert', split_axis=0, concat_axis=0, tiled=True)  145 us
    unnamed x47, local copies, waits for them, and re-layouts  76.8 us
    all_to_all x1, waiting for transfers between devices, move_state(): lax.all_to_all(packed, 'expert', split_axis=0, concat_axis=0, tiled=True)  59 us
    all_to_all x1, waiting for transfers between devices, move_state(): lax.all_to_all(jnp.take(spread, giver, axis=0), 'expert', split_axis=0, c...  58.3 us
    all_to_all x1, waiting for transfers between devices, move_weights(): lax.all_to_all(jnp.take(spread, giver, axis=0), 'expert', split_axis=0, c...  50.3 us
    all_to_all x1, waiting for transfers between devices, move_weights(): lax.all_to_all(packed, 'expert', split_axis=0, concat_axis=0, tiled=True)  33.4 us
    all_gather x1, waiting for transfers between devices, per_device(): hidden_full = lax.all_gather(hidden_part, 'dp', axis=1, tiled=True)  27.8 us
  transfers between devices with their start and end apart: 8, of which 7 were waited for; matrix products, arithmetic and copies ran while one was open for 27% of the time, Pallas kernels for 0%

commit v1 on v0

--- a/solution.py
+++ b/solution.py
@@ -10,6 +10,28 @@
 learn_rate = 0.003
 decay_rate = 0.1
 step_count = 20
+
+
+def joined_along(pieces, dim):
+    shape = list(pieces.shape[1:])
+    shape[dim] *= pieces.shape[0]
+    return jnp.moveaxis(pieces, 0, dim).reshape(shape)
+
+
+def gather_around(shard, axis, dim):
+    size = lax.axis_size(axis)
+    pairs = [(i, (i + 1) % size) for i in range(size)]
+    back = [(b, a) for a, b in pairs]
+    lower, upper = ([], [])
+    for step in range(size - 1):
+        if step % 2 == 0:
+            lower.append(lax.ppermute(lower[-1] if lower else shard, axis, pairs))
+        else:
+            upper.append(lax.ppermute(upper[-1] if upper else shard, axis, back))
+    blocks = jnp.stack([*lower[::-1], shard, *upper])
+    shift = lax.axis_index(axis) - len(lower)
+    blocks = blocks[(jnp.arange(size) - shift) % size]
+    return joined_along(blocks, dim)
 
 
 def dequantize(quant, scale):
@@ -146,7 +168,7 @@
     gate_val = jnp.dot(rows_in, gate_w, preferred_element_type=jnp.float32)
     up_val = jnp.dot(rows_in, up_w, preferred_element_type=jnp.float32)
     hidden_part = (jax.nn.silu(gate_val) * up_val).astype(jnp.bfloat16)
-    hidden_full = lax.all_gather(hidden_part, "dp", axis=1, tiled=True)
+    hidden_full = gather_around(hidden_part, "dp", 1)
     out_total = jnp.dot(hidden_full, down_w, preferred_element_type=jnp.float32)
     grad_total = lax.dot_general(
         hidden_full, back_in, (((0,), (0,)), ((), ())), preferred_element_type=jnp.float32

time: 706 us -> 693 us (0.982)
  waiting for transfers between devices: 384 us -> 358 us
  local copies, waits for them, and re-layouts: 160 us -> 176 us
  between operations: 14.6 us -> 1.35 us
  starting transfers between devices: 66.5 us -> 75.1 us
    all_gather x1 -> x0, waiting for transfers between devices: 27.8 us -> none  [per_device(): hidden_full = lax.all_gather(hidden_part, 'dp', axis=1, tiled=True)]
    ppermute x0 -> x7, starting transfers between devices: none -> 9.26 us  [the longest x3 8.14 us: gather_around(): upper.append(lax.ppermute(upper[-1] if upper else shard, axis, back))]
    unnamed x47 -> x84, local copies, waits for them, and re-layouts: 76.8 us -> 84.2 us
  transfers between devices with their start and end apart: 8 -> 14, of which waited for: 7 -> 8; matrix products, arithmetic and copies ran while one was open for 27% -> 28% of each run, Pallas kernels for 0% -> 0%
where the time goes in v1:
time: 693 us; the launch traced here: 686 us
  waiting for transfers between devices  358 us (52%)
  local copies, waits for them, and re-layouts  176 us (25%)
  starting transfers between devices  75.1 us (11%)
  other arithmetic  37.5 us (5%)
  matrix products  23.5 us (3%)
  blocking collectives  14.3 us (2%)
    all_to_all x1, waiting for transfers between devices, per_device(): lax.all_to_all(sent_rows, 'expert', split_axis=0, concat_axis=0, tiled=True)  148 us
    unnamed x84, local copies, waits for them, and re-layouts  84.2 us
    all_to_all x1, waiting for transfers between devices, move_state(): lax.all_to_all(packed, 'expert', split_axis=0, concat_axis=0, tiled=True)  58.9 us
    all_to_all x1, waiting for transfers between devices, move_state(): lax.all_to_all(jnp.take(spread, giver, axis=0), 'expert', split_axis=0, c...  58.1 us
    all_to_all x1, waiting for transfers between devices, move_weights(): lax.all_to_all(jnp.take(spread, giver, axis=0), 'expert', split_axis=0, c...  50.3 us
    all_to_all x1, waiting for transfers between devices, move_weights(): lax.all_to_all(packed, 'expert', split_axis=0, concat_axis=0, tiled=True)  33.4 us
    all_gather x1, blocking collectives, per_device(): whole_tokens = lax.all_gather(tokens, 'dp', axis=1, tiled=True)  14.3 us
  transfers between devices with their start and end apart: 14, of which 8 were waited for; matrix products, arithmetic and copies ran while one was open for 28% of the time, Pallas kernels for 0%

profile of v1, /device:TPU:2, one launch (start us, length us, event | category | flops | bytes accessed | tf_op | source)
XLA Modules:
  0.0 685.8 jit_solution(148616743044260505)
XLA Ops:
  8.1 3.7 reduce.10
  11.9 5.4 reshape.381
  17.3 11.8 %all-to-all-start.1 = ((bf16[32,2,24576]{2,1,0:T(2,128)(2,1)}), bf16[32,2,24576]{2,1,0:T(2,128)(2,1)S(1)}, u32[]{:S(2)}, u32[]{:S(2)}) async-start(bf16[32,2,24576]{2,1,0:T(2,128)(2,1)} %reshape.381), calls=%async_computation.1 | async-start | bytes 6291456 | tf_op jit(solution)/shard_map/all_to_all | solution.py:85
  29.4 2.7 reshape_reshape.30
  32.2 2.7 reshape_reshape.31
  39.0 9.3 %dynamic-update-slice.11 = f32[32,32771]{1,0:T(8,128)} dynamic-update-slice(f32[32,32771]{1,0:T(8,128)} %dynamic-update-slice.10, f32[32,16384]{1,0:T(8,128)} %reshape_reshape.30, s32[]{} %constant.171, s32[]{} %constant.174) | dynamic-update-slice | bytes 4194308
  48.3 8.7 %dynamic-update-slice.12 = f32[32,32771]{1,0:T(8,128)} dynamic-update-slice(f32[32,32771]{1,0:T(8,128)} %dynamic-update-slice.11, f32[32,16384]{1,0:T(8,128)} %reshape_reshape.31, s32[]{} %constant.171, s32[]{} %constant.179) | dynamic-update-slice | bytes 4194308 | tf_op jit(solution)/shard_map/concatenate | solution.py:68
  57.0 9.8 %all_to_all.43 = f32[32,1,32771]{2,1,0:T(1,128)} reshape(f32[32,32771]{1,0:T(8,128)} %dynamic-update-slice.12) | data formatting | bytes 8389376 | tf_op jit(solution)/shard_map/all_to_all | solution.py:94
  66.9 33.4 %all-to-all-done.1 = bf16[32,2,24576]{2,1,0:T(2,128)(2,1)S(1)} async-done(((bf16[32,2,24576]{2,1,0:T(2,128)(2,1)}), bf16[32,2,24576]{2,1,0:T(2,128)(2,1)S(1)}, u32[]{:S(2)}, u32[]{:S(2)}) %all-to-all-start.1) | async-done | bytes 3145760 | tf_op jit(solution)/shard_map/all_to_all | solution.py:85
  100.3 7.7 %all-to-all-start.3 = ((f32[32,1,32771]{2,1,0:T(1,128)}), f32[32,1,32771]{2,1,0:T(1,128)}, u32[]{:S(2)}, u32[]{:S(2)}) async-start(f32[32,1,32771]{2,1,0:T(1,128)} %all_to_all.43), calls=%async_computation.3 | async-start | bytes 8421376 | tf_op jit(solution)/shard_map/all_to_all | solution.py:94
  108.0 12.5 %reshape.382 = bf16[32,1,49152]{2,1,0:T(2,128)(2,1)} reshape(bf16[32,2,24576]{2,1,0:T(2,128)(2,1)S(1)} %all-to-all-done.1) | data formatting | bytes 6291456
  120.6 6.2 copy.91
  126.8 4.3 gather_fusion.1
  133.3 3.8 reduce.11
  137.1 5.4 reshape.383
  142.5 58.9 %all-to-all-done.3 = f32[32,1,32771]{2,1,0:T(1,128)} async-done(((f32[32,1,32771]{2,1,0:T(1,128)}), f32[32,1,32771]{2,1,0:T(1,128)}, u32[]{:S(2)}, u32[]{:S(2)}) %all-to-all-start.3) | async-done | bytes 4194720 | tf_op jit(solution)/shard_map/all_to_all | solution.py:94
  201.4 8.0 %all-to-all-start.2 = ((bf16[32,2,24576]{2,1,0:T(2,128)(2,1)}), bf16[32,2,24576]{2,1,0:T(2,128)(2,1)}, u32[]{:S(2)}, u32[]{:S(2)}) async-start(bf16[32,2,24576]{2,1,0:T(2,128)(2,1)} %reshape.383), calls=%async_computation.2 | async-start | bytes 6291456 | tf_op jit(solution)/shard_map/all_to_all | solution.py:86
  209.5 4.4 copy.89
  213.9 7.7 %gather_fusion.2 = f32[32,32771]{1,0:T(8,128)} fusion(f32[32,32771]{1,0:T(8,128)} %bitcast.100, s32[1024]{0:T(1024)S(1)} %pad_clamp_fusion.2), kind=kCustom, calls=%fused_computation.2 | custom fusion | bytes 8389504 | tf_op jit(solution)/shard_map/jit(_take)/gather | solution.py:96
  224.1 6.3 copy.63
  230.4 50.3 %all-to-all-done.2 = bf16[32,2,24576]{2,1,0:T(2,128)(2,1)} async-done(((bf16[32,2,24576]{2,1,0:T(2,128)(2,1)}), bf16[32,2,24576]{2,1,0:T(2,128)(2,1)}, u32[]{:S(2)}, u32[]{:S(2)}) %all-to-all-start.2) | async-done | bytes 3145760 | tf_op jit(solution)/shard_map/all_to_all | solution.py:86
  280.6 7.4 %all-to-all-start.4 = ((f32[32,1,32771]{2,1,0:T(1,128)}), f32[32,1,32771]{2,1,0:T(1,128)}, u32[]{:S(2)}, u32[]{:S(2)}) async-start(f32[32,1,32771]{2,1,0:T(1,128)} %copy.63), calls=%async_computation.4 | async-start | bytes 8421376 | tf_op jit(solution)/shard_map/all_to_all | solution.py:95
  290.5 3.4 scatter_custom_fusion
  294.0 14.3 %all_gather.3 = bf16[96,4096]{1,0:T(8,128)(2,1)S(1)} all-gather(bf16[96,512]{1,0:T(8,128)(2,1)S(1)} %copy-done.13), channel_id=1, replica_groups=mesh['expert'=32,'dp'=8] {'dp'}, dimensions={1}, use_global_device_ids=true | all-gather | bytes 884736 | tf_op jit(solution)/shard_map/all_gather | solution.py:156
  308.4 7.8 %gather_fusion = bf16[1024,4096]{1,0:T(8,128)(2,1)} fusion(bf16[96,4096]{1,0:T(8,128)(2,1)S(1)} %all_gather.3, s32[1024]{0:T(1024)S(1)} %get-tuple-element.17), kind=kCustom, calls=%fused_computation | custom fusion | bytes 16781312 | tf_op jit(solution)/shard_map/jit(_take)/gather | solution.py:157
  316.2 7.4 %broadcast_select_fusion = bf16[32,32,4096]{2,1,0:T(8,128)(2,1)} fusion(bf16[32,32,4096]{2,1,0:T(8,128)(2,1)} %bitcast.103, pred[32,32]{1,0:T(8,128)(4,1)S(1)} %broadcast_in_dim.104), kind=kLoop, calls=%fused_computation.8 | loop fusion | flops 4194304 | bytes 16778240 | tf_op jit(solution)/shard_map/jit(_take)/select_n | solution.py:157
  323.6 58.1 %all-to-all-done.4 = f32[32,1,32771]{2,1,0:T(1,128)} async-done(((f32[32,1,32771]{2,1,0:T(1,128)}), f32[32,1,32771]{2,1,0:T(1,128)}, u32[]{:S(2)}, u32[]{:S(2)}) %all-to-all-start.4) | async-done | bytes 4194720 | tf_op jit(solution)/shard_map/all_to_all | solution.py:95
  381.6 7.6 %all-to-all-start = ((bf16[32,32,4096]{2,1,0:T(8,128)(2,1)}), bf16[32,32,4096]{2,1,0:T(8,128)(2,1)}, u32[]{:S(2)}, u32[]{:S(2)}) async-start(bf16[32,32,4096]{2,1,0:T(8,128)(2,1)} %broadcast_select_fusion), calls=%async_computation | async-start | bytes 16777216 | tf_op jit(solution)/shard_map/all_to_all | solution.py:159
  389.5 4.5 gather_fusion.5
  394.7 4.0 gather_fusion.6
  398.7 19.0 %reshape.384 = bf16[32,1,49152]{2,1,0:T(2,128)(2,1)} reshape(bf16[32,2,24576]{2,1,0:T(2,128)(2,1)} %all-to-all-done.2) | data formatting | bytes 6291456
  417.7 6.2 copy.90
  423.9 3.6 copy.88
  432.0 147.6 %all-to-all-done = bf16[32,32,4096]{2,1,0:T(8,128)(2,1)} async-done(((bf16[32,32,4096]{2,1,0:T(8,128)(2,1)}), bf16[32,32,4096]{2,1,0:T(8,128)(2,1)}, u32[]{:S(2)}, u32[]{:S(2)}) %all-to-all-start) | async-done | bytes 8388640 | tf_op jit(solution)/shard_map/all_to_all | solution.py:159
  579.6 5.8 fusion.18
  585.4 5.7 fusion.1
  592.6 13.5 %all-to-all-start.6 = ((bf16[32,32,512]{2,1,0:T(8,128)(2,1)}), bf16[32,32,512]{2,1,0:T(8,128)(2,1)}, u32[]{:S(2)}, u32[]{:S(2)}) async-start(bf16[32,32,512]{2,1,0:T(8,128)(2,1)} %multiply_convert_fusion), calls=%async_computation.6 | async-start | bytes 2097152 | tf_op jit(solution)/shard_map/all_to_all | solution.py:160
  611.0 2.7 collective-permute-done.1
  619.2 2.9 collective-permute-start.5
  622.2 2.7 multiply_convert_fusion.1
  626.3 3.4 collective-permute-start.6
  642.7 3.8 convolution_convert_fusion
  646.5 9.8 %all-to-all-start.5 = ((bf16[32,32,512]{2,1,0:T(8,128)(2,1)}), bf16[32,32,512]{2,1,0:T(8,128)(2,1)S(1)}, u32[]{:S(2)}, u32[]{:S(2)}) async-start(bf16[32,32,512]{2,1,0:T(8,128)(2,1)} %bitcast.23), calls=%async_computation.5 | async-start | bytes 2097152 | tf_op jit(solution)/shard_map/all_to_all | solution.py:177
  656.3 4.7 slice_multiply_fusion
  661.0 2.7 mul.149
  667.6 8.1 %fusion.6 = (f32[1,1024,512]{2,1,0:T(8,128)}, bf16[1,1024,512]{2,1,0:T(8,128)(2,1)}, f32[1,1024,512]{2,1,0:T(8,128)}) fusion(f32[1024,512]{1,0:T(8,128)} %mul.156, f32[1024,512]{1,0:T(8,128)} %mul.149, f32[1024,512]{1,0:T(8,128)S(1)} %copy-done.4, f32[128,8,4,128]{3,2,1,0:T(4,128)S(1)} %bitcast.112, bf16[1024,1024]{0,1:T(8,128)(2,1)} %bitcast.114, ...), kind=kOutput, calls=%fused_computation.37 | convolution fusion | flops 1081606144 | bytes 16777216 | tf_op jit(solution)/shard_map/dot_general | solution.py:173
  675.7 5.9 all-to-all-done.5
  681.7 2.7 gather_fusion.4
  (139 shorter events, 56.0 us)
Async XLA Ops:
  0.6 394.1 %copy-start = (bf16[96,512]{1,0:T(8,128)(2,1)S(1)}, bf16[96,512]{1,0:T(8,128)(2,1)}, u32[]{:S(2)}) copy-start(bf16[96,512]{1,0:T(8,128)(2,1)} %param.17) | copy-start | bytes 294916
  0.6 2.5 copy-start.5
  0.7 3.7 copy-start.6
  17.3 11.8 %copy-start.27 = (f32[1,32,1]{1,2,0:T(1,128)S(1)}, f32[1,32,1]{1,2,0:T(1,128)}, u32[]{:S(2)}) copy-start(f32[1,32,1]{1,2,0:T(1,128)} %param.20) | copy-start | bytes 388
  17.3 11.9 %copy-start.28 = (f32[1,32,1]{1,2,0:T(1,128)S(1)}, f32[1,32,1]{1,2,0:T(1,128)}, u32[]{:S(2)}) copy-start(f32[1,32,1]{1,2,0:T(1,128)} %param.21) | copy-start | bytes 388
  17.3 12.0 %copy-start.26 = (f32[1,8,4]{1,2,0:T(4,128)S(1)}, f32[1,8,4]{1,2,0:T(4,128)}, u32[]{:S(2)}) copy-start(f32[1,8,4]{1,2,0:T(4,128)} %param.23) | copy-start | bytes 388
  17.3 83.0 %all-to-all-start.1 = ((bf16[32,2,24576]{2,1,0:T(2,128)(2,1)}), bf16[32,2,24576]{2,1,0:T(2,128)(2,1)S(1)}, u32[]{:S(2)}, u32[]{:S(2)}) async-start(bf16[32,2,24576]{2,1,0:T(2,128)(2,1)} %reshape.381), calls=%async_computation.1 | async-start | bytes 6291456 | tf_op jit(solution)/shard_map/all_to_all | solution.py:85
  57.0 9.8 %copy-start.29 = (s32[32]{0:T(128)S(1)}, s32[32]{0:T(128)}, u32[]{:S(2)}) copy-start(s32[32]{0:T(128)} %param.27) | copy-start | bytes 388
  57.0 9.8 %copy-start.30 = (s32[32]{0:T(128)S(1)}, s32[32]{0:T(128)}, u32[]{:S(2)}) copy-start(s32[32]{0:T(128)} %param.26) | copy-start | bytes 388
  100.3 101.1 %all-to-all-start.3 = ((f32[32,1,32771]{2,1,0:T(1,128)}), f32[32,1,32771]{2,1,0:T(1,128)}, u32[]{:S(2)}, u32[]{:S(2)}) async-start(f32[32,1,32771]{2,1,0:T(1,128)} %all_to_all.43), calls=%async_computation.3 | async-start | bytes 8421376 | tf_op jit(solution)/shard_map/all_to_all | solution.py:94
  201.4 79.2 %all-to-all-start.2 = ((bf16[32,2,24576]{2,1,0:T(2,128)(2,1)}), bf16[32,2,24576]{2,1,0:T(2,128)(2,1)}, u32[]{:S(2)}, u32[]{:S(2)}) async-start(bf16[32,2,24576]{2,1,0:T(2,128)(2,1)} %reshape.383), calls=%async_computation.2 | async-start | bytes 6291456 | tf_op jit(solution)/shard_map/all_to_all | solution.py:86
  230.4 57.6 %copy-start.23 = (s32[96,8]{0,1:T(8,128)S(1)}, s32[96,8]{0,1:T(8,128)}, u32[]{:S(2)}) copy-start(s32[96,8]{0,1:T(8,128)} %param.16) | copy-start | bytes 9220
  230.4 63.7 %copy-start.13 = (bf16[96,512]{1,0:T(8,128)(2,1)S(1)}, bf16[96,512]{1,0:T(8,128)(2,1)}, u32[]{:S(2)}) copy-start(bf16[96,512]{1,0:T(8,128)(2,1)} %param.14) | copy-start | bytes 294916
  280.6 101.0 %all-to-all-start.4 = ((f32[32,1,32771]{2,1,0:T(1,128)}), f32[32,1,32771]{2,1,0:T(1,128)}, u32[]{:S(2)}, u32[]{:S(2)}) async-start(f32[32,1,32771]{2,1,0:T(1,128)} %copy.63), calls=%async_computation.4 | async-start | bytes 8421376 | tf_op jit(solution)/shard_map/all_to_all | solution.py:95
  290.5 3.5 copy-start.18
  290.5 3.5 copy-start.21
  294.0 22.1 %copy-start.16 = (pred[32,32]{1,0:T(8,128)(4,1)}, pred[32,32]{1,0:T(8,128)(4,1)S(1)}, u32[]{:S(2)}) copy-start(pred[32,32]{1,0:T(8,128)(4,1)S(1)} %broadcast_in_dim.104) | copy-start | bytes 3076
  323.6 65.7 %copy-start.24 = (f32[96,8]{0,1:T(8,128)S(1)}, f32[96,8]{0,1:T(8,128)}, u32[]{:S(2)}) copy-start(f32[96,8]{0,1:T(8,128)} %param.15) | copy-start | bytes 9220
  381.6 198.0 %all-to-all-start = ((bf16[32,32,4096]{2,1,0:T(8,128)(2,1)}), bf16[32,32,4096]{2,1,0:T(8,128)(2,1)}, u32[]{:S(2)}, u32[]{:S(2)}) async-start(bf16[32,32,4096]{2,1,0:T(8,128)(2,1)} %broadcast_select_fusion), calls=%async_computation | async-start | bytes 16777216 | tf_op jit(solution)/shard_map/all_to_all | solution.py:159
  423.9 4.5 copy-start.2
  427.5 2.0 copy-start.1
  430.7 148.9 %copy-start.7 = (bf16[4096,128]{1,0:T(8,128)(2,1)S(1)}, bf16[4096,128]{1,0:T(8,128)(2,1)}, u32[]{:S(2)}) copy-start(bf16[4096,128]{1,0:T(8,128)(2,1)} %convert_element_type.87) | copy-start | bytes 3145732
  579.6 5.8 copy-start.8
  585.4 5.8 copy-start.14
  585.4 5.8 copy-start.17
  591.1 15.6 %collective-permute-start = (bf16[1024,128]{1,0:T(8,128)(2,1)S(1)}, bf16[1024,128]{1,0:T(8,128)(2,1)S(1)}, u32[]{:S(2)}, u32[]{:S(2)}) collective-permute-start(bf16[1024,128]{1,0:T(8,128)(2,1)S(1)} %fusion.1), channel_id=1, source_target_pairs={{0,1},{1,2},{2,3},{3,4},{4,5},{5,6},{6,7},{7,0},{8,9},{9,10},{10,1... | collective-permute-start | bytes 786440 | tf_op jit(solution)/shard_map/ppermute | solution.py:28
  591.2 14.9 %copy-start.22 = (s32[768]{0:T(1024)S(1)}, s32[768]{0:T(1024)}, u32[]{:S(2)}) copy-start(s32[768]{0:T(1024)} %copy-done.21) | copy-start | bytes 9220
  591.2 17.2 %copy-start.19 = (s32[768]{0:T(1024)S(1)}, s32[768]{0:T(1024)}, u32[]{:S(2)}) copy-start(s32[768]{0:T(1024)} %copy-done.18) | copy-start | bytes 9220
  592.6 54.0 %all-to-all-start.6 = ((bf16[32,32,512]{2,1,0:T(8,128)(2,1)}), bf16[32,32,512]{2,1,0:T(8,128)(2,1)}, u32[]{:S(2)}, u32[]{:S(2)}) async-start(bf16[32,32,512]{2,1,0:T(8,128)(2,1)} %multiply_convert_fusion), calls=%async_computation.6 | async-start | bytes 2097152 | tf_op jit(solution)/shard_map/all_to_all | solution.py:160
  606.7 7.0 %copy-start.9 = (bf16[1024,128]{1,0:T(8,128)(2,1)}, bf16[1024,128]{1,0:T(8,128)(2,1)S(1)}, u32[]{:S(2)}) copy-start(bf16[1024,128]{1,0:T(8,128)(2,1)S(1)} %collective-permute-done) | copy-start | bytes 786436
  606.7 7.0 %collective-permute-start.1 = (bf16[1024,128]{1,0:T(8,128)(2,1)S(1)}, bf16[1024,128]{1,0:T(8,128)(2,1)S(1)}, u32[]{:S(2)}, u32[]{:S(2)}) collective-permute-start(bf16[1024,128]{1,0:T(8,128)(2,1)S(1)} %collective-permute-done), channel_id=1, source_target_pairs={{0,1},{1,2},{2,3},{3,4},{4,5},{5,6},{6,7},{7,0},{8,9},{9,10},{10,1... | collective-permute-start | bytes 786440 | tf_op jit(solution)/shard_map/ppermute | solution.py:28
  609.1 10.1 %collective-permute-start.4 = (bf16[1024,128]{1,0:T(8,128)(2,1)S(1)}, bf16[1024,128]{1,0:T(8,128)(2,1)}, u32[]{:S(2)}, u32[]{:S(2)}) collective-permute-start(bf16[1024,128]{1,0:T(8,128)(2,1)S(1)} %fusion.1), channel_id=1, source_target_pairs={{1,0},{2,1},{3,2},{4,3},{5,4},{6,5},{7,6},{0,7},{9,8},{10,9},{11,1... | collective-permute-start | bytes 786440 | tf_op jit(solution)/shard_map/ppermute | solution.py:30
  613.7 3.0 copy-start.11
  613.7 8.4 %collective-permute-start.2 = (bf16[1024,128]{1,0:T(8,128)(2,1)S(1)}, bf16[1024,128]{1,0:T(8,128)(2,1)}, u32[]{:S(2)}, u32[]{:S(2)}) collective-permute-start(bf16[1024,128]{1,0:T(8,128)(2,1)S(1)} %collective-permute-done.1), channel_id=1, source_target_pairs={{0,1},{1,2},{2,3},{3,4},{4,5},{5,6},{6,7},{7,0},{8,9},{9,10},{10,1... | collective-permute-start | bytes 786440 | tf_op jit(solution)/shard_map/ppermute | solution.py:28
  616.8 2.4 copy-start.25
  619.2 7.1 %collective-permute-start.5 = (bf16[1024,128]{1,0:T(8,128)(2,1)}, bf16[1024,128]{1,0:T(8,128)(2,1)S(1)}, u32[]{:S(2)}, u32[]{:S(2)}) collective-permute-start(bf16[1024,128]{1,0:T(8,128)(2,1)} %collective-permute-done.4), channel_id=1, source_target_pairs={{1,0},{2,1},{3,2},{4,3},{5,4},{6,5},{7,6},{0,7},{9,8},{10,9},{11,1... | collective-permute-start | bytes 786440 | tf_op jit(solution)/shard_map/ppermute | solution.py:30
  622.1 7.6 %collective-permute-start.3 = (bf16[1024,128]{1,0:T(8,128)(2,1)}, bf16[1024,128]{1,0:T(8,128)(2,1)S(1)}, u32[]{:S(2)}, u32[]{:S(2)}) collective-permute-start(bf16[1024,128]{1,0:T(8,128)(2,1)} %collective-permute-done.2), channel_id=1, source_target_pairs={{0,1},{1,2},{2,3},{3,4},{4,5},{5,6},{6,7},{7,0},{8,9},{9,10},{10,1... | collective-permute-start | bytes 786440 | tf_op jit(solution)/shard_map/ppermute | solution.py:28
  622.2 8.3 %copy-start.3 = (f32[8,128,4]{2,1,0:T(8,128)}, f32[8,128,4]{2,1,0:T(8,128)S(1)}, u32[]{:S(2)}) copy-start(f32[8,128,4]{2,1,0:T(8,128)S(1)} %broadcast_in_dim.112) | copy-start | bytes 49156
  622.2 10.0 %copy-start.12 = (bf16[1024,128]{1,0:T(8,128)(2,1)S(1)}, bf16[1024,128]{1,0:T(8,128)(2,1)}, u32[]{:S(2)}) copy-start(bf16[1024,128]{1,0:T(8,128)(2,1)} %copy-done.11) | copy-start | bytes 786436
  622.2 10.7 %copy-start.10 = (bf16[1024,128]{1,0:T(8,128)(2,1)S(1)}, bf16[1024,128]{1,0:T(8,128)(2,1)}, u32[]{:S(2)}) copy-start(bf16[1024,128]{1,0:T(8,128)(2,1)} %copy-done.9) | copy-start | bytes 786436
  626.3 10.4 %collective-permute-start.6 = (bf16[1024,128]{1,0:T(8,128)(2,1)S(1)}, bf16[1024,128]{1,0:T(8,128)(2,1)S(1)}, u32[]{:S(2)}, u32[]{:S(2)}) collective-permute-start(bf16[1024,128]{1,0:T(8,128)(2,1)S(1)} %collective-permute-done.5), channel_id=1, source_target_pairs={{1,0},{2,1},{3,2},{4,3},{5,4},{6,5},{7,6},{0,7},{9,8},{10,9},{11,1... | collective-permute-start | bytes 786440 | tf_op jit(solution)/shard_map/ppermute | solution.py:30
  646.5 35.1 %all-to-all-start.5 = ((bf16[32,32,512]{2,1,0:T(8,128)(2,1)}), bf16[32,32,512]{2,1,0:T(8,128)(2,1)S(1)}, u32[]{:S(2)}, u32[]{:S(2)}) async-start(bf16[32,32,512]{2,1,0:T(8,128)(2,1)} %bitcast.23), calls=%async_computation.5 | async-start | bytes 2097152 | tf_op jit(solution)/shard_map/all_to_all | solution.py:177
  665.2 2.3 copy-start.4
  667.6 14.1 %copy-start.20 = (s32[1024]{0:T(1024)S(1)}, s32[1024]{0:T(1024)}, u32[]{:S(2)}) copy-start(s32[1024]{0:T(1024)} %pad_clamp_fusion) | copy-start | bytes 12292
  681.7 2.7 copy-start.15
